TPU v7x, 32 devices: a whole 2x2x4 slice. The times are simulated.
32 devices in a mesh: row: 8 (over z, y), col: 4 (over x, core).
Axes of the slice: x: 2, y: 2, z: 4, core: 2. Of those that a mesh axis runs over, the one named last changes fastest.
Arguments:
- amplitudes_right: float32 [8, 2048], P(None, ('row', 'col')), may hold values from -5 to 5
- amplitudes_left: float32 [8, 2048], P(None, ('row', 'col')), may hold values from -7 to 7
- previous_right: float32 [8, 2048], P(None, ('row', 'col')), may hold values from -6 to 6
- previous_left: float32 [8, 2048], P(None, ('row', 'col')), may hold values from -6 to 6
- coupling: float32 [2, 8], replicated, may hold values from 0.2 to 1
- ladder: bfloat16 [2048, 2048], P('row', 'col'), may hold values from -1 to 5
Outputs:
- next_right: float32 [8, 2048], P(None, ('row', 'col'))
- next_left: float32 [8, 2048], P(None, ('row', 'col'))
- coefficients: float32 [3, 8], replicated
All inputs are finite; a program needn't handle non-finite values.
Results may differ from a plain program's by a relative error of at most 0.003.
Values may be sent and summed in bfloat16 or wider, within the bound.
A program may use at most 64 MiB of HBM per device.

v0:
```python
import functools

import jax
import jax.numpy as jnp
from jax import lax
from jax.experimental import pallas as pl
from jax.experimental.pallas import tpu as pltpu
from jax.sharding import PartitionSpec as P

MESH = pl.DeviceIdType.MESH
LANES = 128
UNROLL_MOST = 32
SMALLEST_SQUARE = 1e-12


def each(count, body):
    if count <= UNROLL_MOST:
        for i in range(count):
            body(i)
    else:
        lax.fori_loop(0, count, lambda i, carry: (body(i), carry)[1], 0)


def arrived(ref, count, sem):
    part = ref.at[pl.ds(0, count)]
    pltpu.make_async_copy(part, part, sem).wait()


def kernel(
    rows_count,
    cols_count,
    right_in,
    left_in,
    prev_right_in,
    prev_left_in,
    coupling_in,
    ladder_in,
    next_right_out,
    next_left_out,
    coefficients_out,
    right_own,
    left_own,
    prev_right_own,
    prev_left_own,
    coupling_own,
    ladder_own,
    right_sent,
    left_sent,
    right_got,
    left_got,
    right_part,
    left_part,
    right_part_got,
    left_part_got,
    sums_sent,
    sums_got,
    load_sem,
    send_sem,
    recv_sem,
):
    devices = rows_count * cols_count
    depth, share = right_own.shape
    pack = LANES // share
    pairs_total = share * devices
    my_row = lax.axis_index("row")
    my_col = lax.axis_index("col")
    me = my_row * cols_count + my_col
    home_col = lax.div(me, rows_count)
    home_slot = lax.rem(me, rows_count)
    at_home = home_col == my_col

    loads = [
        pltpu.make_async_copy(src, dst, load_sem.at[i])
        for i, (src, dst) in enumerate(
            (
                (right_in, right_own),
                (left_in, left_own),
                (prev_right_in, prev_right_own),
                (prev_left_in, prev_left_own),
                (coupling_in, coupling_own),
                (ladder_in, ladder_own),
            )
        )
    ]
    for load in loads:
        load.start()

    def at(device):
        return (lax.div(device, cols_count), lax.rem(device, cols_count))

    def peer(i):
        return (my_row, lax.rem(my_col + i + 1, cols_count))

    def holder(i):
        return at(my_col * rows_count + lax.rem(home_slot + i, rows_count))

    def user(i):
        return (lax.rem(my_row + i, rows_count), home_col)

    def unless_me(i, go):
        if i == 0:
            pl.when(jnp.logical_not(at_home))(go)
        else:
            go()

    barrier = pltpu.get_barrier_semaphore()

    def greet(device):
        pl.semaphore_signal(barrier, inc=1, device_id=device, device_id_type=MESH)

    for i in range(rows_count):
        unless_me(i, lambda: greet(holder(i)))
        unless_me(i, lambda: greet(user(i)))
    for i in range(cols_count - 1):
        greet(peer(i))

    lane = lax.broadcasted_iota(jnp.int32, (depth, LANES), 1)
    sub = lax.broadcasted_iota(jnp.int32, (depth, LANES), 0)
    mine = lane // share == lax.rem(my_col, pack)

    def spread(array):
        return jnp.where(mine, jnp.concatenate([array] * pack, axis=1), 0.0)

    def to_lanes(columns):
        row = jnp.zeros((depth, LANES), jnp.float32)
        for i, column in enumerate(columns):
            row = row + jnp.where(lane == sub + i * depth, column, 0.0)
        return jnp.sum(row, axis=0, keepdims=True)

    def to_column(row, i):
        return jnp.sum(jnp.where(lane == sub + i * depth, row, 0.0), axis=1, keepdims=True)

    loads[0].wait()
    loads[1].wait()
    right = spread(right_own[...])
    left = spread(left_own[...])
    right_sent[0] = right
    left_sent[0] = left
    left_got[pl.ds(my_col, 1)] = left[None]

    @pl.when(at_home)
    def _():
        right_got[pl.ds(home_slot, 1)] = right[None]

    pl.semaphore_wait(barrier, 2 * rows_count + cols_count - 1 - 2 * at_home.astype(jnp.int32))

    def send(src, dst, sems, device):
        pltpu.make_async_remote_copy(
            src_ref=src,
            dst_ref=dst,
            send_sem=send_sem.at[sems],
            recv_sem=recv_sem.at[sems],
            device_id=device,
            device_id_type=MESH,
        ).start()

    for i in (*range(1, rows_count), 0):
        unless_me(i, lambda: send(right_sent.at[0], right_got.at[home_slot], 0, user(i)))
    for i in range(cols_count - 1):
        send(left_sent.at[0], left_got.at[my_col], 1, peer(i))

    for load in loads[2:]:
        load.wait()
    coupling_row = coupling_own[...]
    near = lax.broadcasted_iota(jnp.int32, (depth, depth), 0) == lax.broadcasted_iota(
        jnp.int32, (depth, depth), 1
    )

    def coefficient(i):
        return jnp.sum(jnp.where(near, coupling_row[i : i + 1], 0.0), axis=1, keepdims=True)

    right_base = coefficient(1) * spread(prev_right_own[...])
    left_base = coefficient(0) * spread(prev_left_own[...])

    def joined(ref, count):
        return jnp.concatenate(
            [sum(ref[i * pack + j] for j in range(pack)) for i in range(count // pack)], axis=1
        )

    arrived(left_got, cols_count - 1, recv_sem.at[1])
    left_rows = joined(left_got, cols_count)
    left_terms = jnp.dot(
        left_rows.astype(jnp.bfloat16), ladder_own[...], preferred_element_type=jnp.float32
    )
    for i in range(rows_count // pack):
        left_part[i] = left_terms[:, i * LANES : (i + 1) * LANES]

    for i in (*range(1, rows_count), 0):
        chunk = lax.div(lax.rem(home_slot + i, rows_count), pack)
        unless_me(
            i, lambda: send(left_part.at[chunk], left_part_got.at[my_row], 2, holder(i))
        )

    @pl.when(at_home)
    def _():
        left_part_got[pl.ds(my_row, 1)] = left_part[pl.ds(lax.div(home_slot, pack), 1)]
        arrived(right_got, rows_count - 1, recv_sem.at[0])

    @pl.when(jnp.logical_not(at_home))
    def _():
        arrived(right_got, rows_count, recv_sem.at[0])

    right_cols = joined(right_got, rows_count)
    right_terms = lax.dot_general(
        right_cols.astype(jnp.bfloat16),
        ladder_own[...],
        (((1,), (1,)), ((), ())),
        preferred_element_type=jnp.float32,
    )
    for i in range(cols_count // pack):
        right_part[i] = right_terms[:, i * LANES : (i + 1) * LANES]

    for i in range(cols_count - 1):
        chunk = lax.div(lax.rem(my_col + i + 1, cols_count), pack)
        send(right_part.at[chunk], right_part_got.at[my_col], 3, peer(i))
    right_part_got[pl.ds(my_col, 1)] = right_part[pl.ds(lax.div(my_col, pack), 1)]

    def inner(first, second):
        return jnp.sum(first * second, axis=1, keepdims=True)

    def fitted(product, square):
        usable = square > SMALLEST_SQUARE
        return jnp.where(usable, product / jnp.where(usable, square, 1.0), 0.0)

    right_square = inner(right, right)
    left_square = inner(left, left)
    left_right = inner(left, right)

    arrived(right_part_got, cols_count - 1, recv_sem.at[3])
    image_right = jnp.where(mine, jnp.sum(right_part_got[...], axis=0), 0.0)
    alpha_part = inner(left, image_right)
    right_base = image_right - right_base
    right_fit = fitted(inner(right_base, right), right_square)
    right_rest = right_base - right_fit * right

    @pl.when(at_home)
    def _():
        arrived(left_part_got, rows_count - 1, recv_sem.at[2])

    @pl.when(jnp.logical_not(at_home))
    def _():
        arrived(left_part_got, rows_count, recv_sem.at[2])

    left_base = jnp.where(mine, jnp.sum(left_part_got[...], axis=0), 0.0) - left_base
    left_fit = fitted(inner(left_base, left), left_square)
    left_rest = left_base - left_fit * left

    sums_sent[...] = to_lanes(
        [
            alpha_part,
            right_fit,
            left_fit,
            inner(right_rest, right_rest),
            inner(right_rest, right),
            right_square,
            inner(left_rest, left_rest),
            inner(left_rest, left),
            left_square,
            inner(left_rest, right_rest),
            inner(left_rest, right),
            inner(left, right_rest),
            left_right,
        ]
    )
    each(
        devices - 1,
        lambda i: send(
            sums_sent, sums_got.at[pl.ds(me, 1)], 4, at(lax.rem(me + i + 1, devices))
        ),
    )
    sums_got[pl.ds(me, 1)] = sums_sent[...]

    arrived(right_got, rows_count - 1, send_sem.at[0])
    arrived(left_got, cols_count - 1, send_sem.at[1])
    arrived(left_part_got, rows_count - 1, send_sem.at[2])
    arrived(right_part_got, cols_count - 1, send_sem.at[3])

    @pl.when(jnp.logical_not(at_home))
    def _():
        arrived(right_got, 1, send_sem.at[0])
        arrived(left_part_got, 1, send_sem.at[2])

    arrived(sums_got, devices - 1, recv_sem.at[4])
    sums = sums_got[...]

    def value(i):
        return pltpu.roll(sums, LANES - i * depth, 1)

    def total(values):
        return jnp.sum(values, axis=0, keepdims=True) / pairs_total

    alpha_row = total(sums)
    right_off = value(1) - alpha_row
    left_off = value(2) - alpha_row
    right_norm = to_column(
        total(value(3) + right_off * (2.0 * value(4) + right_off * value(5))), 0
    )
    left_norm = to_column(total(value(6) + left_off * (2.0 * value(7) + left_off * value(8))), 0)
    omega_val = to_column(
        total(
            value(9)
            + right_off * value(10)
            + left_off * value(11)
            + right_off * left_off * value(12)
        ),
        0,
    )
    alpha_now = to_column(alpha_row, 0)
    right_res = right_base - alpha_now * right
    left_res = left_base - alpha_now * left
    safe_omega = jnp.maximum(jnp.abs(omega_val), 0.1 * jnp.sqrt(right_norm * left_norm + 1e-06))
    beta_new = jnp.sqrt(safe_omega)
    gamma_new = omega_val / beta_new

    def own_part(array):
        out = array[:, :share]
        for i in range(1, pack):
            out = jnp.where(
                lax.rem(my_col, pack) == i, array[:, i * share : (i + 1) * share], out
            )
        return out

    next_right_out[...] = own_part(right_res / beta_new)
    next_left_out[...] = own_part(left_res * (gamma_new / safe_omega))
    coefficients_out[0:1] = alpha_row[:, :depth]
    coefficients_out[1:2] = to_lanes([beta_new])[:, :depth]
    coefficients_out[2:3] = to_lanes([gamma_new])[:, :depth]
    arrived(sums_got, devices - 1, send_sem.at[4])


def store(a_in, b_in, c_in, a_out, b_out, c_out, sem):
    copies = [
        pltpu.make_async_copy(src, dst, sem.at[i])
        for i, (src, dst) in enumerate(((a_in, a_out), (b_in, b_out), (c_in, c_out)))
    ]
    for copy in copies:
        copy.start()
    for copy in copies:
        copy.wait()


def local(rows_count, cols_count, right, left, prev_right, prev_left, coupling, ladder):
    depth, share = right.shape
    devices = rows_count * cols_count
    pack = LANES // share
    f32 = jnp.float32
    vec = pltpu.VMEM((depth, share), f32)

    def tiles(count):
        return pltpu.VMEM((count, depth, LANES), f32)

    results = pl.pallas_call(
        functools.partial(kernel, rows_count, cols_count),
        out_shape=(
            jax.ShapeDtypeStruct(right.shape, f32),
            jax.ShapeDtypeStruct(left.shape, f32),
            jax.ShapeDtypeStruct((3, depth), f32),
        ),
        in_specs=[pl.BlockSpec(memory_space=pltpu.HBM)] * 6,
        out_specs=(pl.BlockSpec(memory_space=pltpu.VMEM),) * 3,
        scratch_shapes=[
            vec,
            vec,
            vec,
            vec,
            pltpu.VMEM(coupling.shape, f32),
            pltpu.VMEM(ladder.shape, ladder.dtype),
            tiles(1),
            tiles(1),
            tiles(rows_count),
            tiles(cols_count),
            tiles(cols_count // pack),
            tiles(rows_count // pack),
            tiles(cols_count),
            tiles(rows_count),
            pltpu.VMEM((1, LANES), f32),
            pltpu.VMEM((devices, LANES), f32),
            pltpu.SemaphoreType.DMA((6,)),
            pltpu.SemaphoreType.DMA((5,)),
            pltpu.SemaphoreType.DMA((5,)),
        ],
        compiler_params=pltpu.CompilerParams(
            collective_id=0, has_side_effects=True, vmem_limit_bytes=56 * 1024 * 1024
        ),
    )(right, left, prev_right, prev_left, coupling, ladder)
    return pl.pallas_call(
        store,
        out_shape=tuple(jax.ShapeDtypeStruct(x.shape, x.dtype) for x in results),
        in_specs=[pl.BlockSpec(memory_space=pltpu.HBM)] * 3,
        out_specs=(pl.BlockSpec(memory_space=pltpu.HBM),) * 3,
        scratch_shapes=[pltpu.SemaphoreType.DMA((3,))],
        compiler_params=pltpu.CompilerParams(vmem_limit_bytes=56 * 1024 * 1024),
    )(*results)


def solution(mesh):
    vector = P(None, ("row", "col"))
    return jax.shard_map(
        functools.partial(local, mesh.shape["row"], mesh.shape["col"]),
        mesh=mesh,
        in_specs=(vector, vector, vector, vector, P(), P("row", "col")),
        out_specs=(vector, vector, P()),
        check_vma=False,
    )
```

profile of v0, /device:TPU:0, one launch (start us, length us, event | category | flops | bytes accessed | tf_op | source)
XLA Modules:
  0.0 21.7 jit_solution(14909653352131659689)
XLA Ops:
  0.6 19.7 %shard_map.85 = (f32[8,64]{1,0:T(8,128)}, f32[8,64]{1,0:T(8,128)}, f32[3,8]{1,0:T(4,128)}) custom-call(f32[8,64]{1,0:T(8,128)} %right_in.1, f32[8,64]{1,0:T(8,128)} %left_in.1, f32[8,64]{1,0:T(8,128)} %prev_right_in.1, f32[8,64]{1,0:T(8,128)} %prev_left_in.1, f32[2,8]{1,0:T(2,128)} %coupling_in.1, bf16[256,512]{1,0:T(8,128)(2,1)} %ladder_in.1), custom_call_target="tpu_custom_call" | custom-call | tf_op jit(solution)/shard_map/pallas_call | solution.py:352
  20.3 1.4 %shard_map.86 = (f32[8,64]{1,0:T(8,128)}, f32[8,64]{1,0:T(8,128)}, f32[3,8]{1,0:T(4,128)}) custom-call(f32[8,64]{1,0:T(8,128)} %get-tuple-element.6.a_in, f32[8,64]{1,0:T(8,128)} %get-tuple-element.7.b_in, f32[3,8]{1,0:T(4,128)} %get-tuple-element.8.c_in), custom_call_target="tpu_custom_call" | custom-call | tf_op jit(solution)/shard_map/pallas_call | solution.py:386
where the time goes:
time: 21.9 us; the launch traced here: 21.7 us
  Pallas kernels  21.1 us (96%)
  between operations  0.64 us (3%)
    pallas_call x1, Pallas kernels, local(): pl.pallas_call(functools.partial(kernel, rows_count, cols_count), out_sha...  19.7 us
    pallas_call x1, Pallas kernels, local(): pl.pallas_call(store, out_shape=tuple((jax.ShapeDtypeStruct(x.shape, x.dt...  1.43 us

commit v1 on v0

--- a/solution.py
+++ b/solution.py
@@ -38,16 +38,11 @@
     next_right_out,
     next_left_out,
     coefficients_out,
-    right_own,
-    left_own,
-    prev_right_own,
-    prev_left_own,
     coupling_own,
     ladder_own,
-    right_sent,
-    left_sent,
     right_got,
     left_got,
+    mates_got,
     right_part,
     left_part,
     right_part_got,
@@ -59,7 +54,7 @@
     recv_sem,
 ):
     devices = rows_count * cols_count
-    depth, share = right_own.shape
+    depth, share = right_in.shape
     pack = LANES // share
     pairs_total = share * devices
     my_row = lax.axis_index("row")
@@ -69,21 +64,23 @@
     home_slot = lax.rem(me, rows_count)
     at_home = home_col == my_col
 
+    groups = devices // pack
+    my_group = lax.div(me, pack)
+    my_sub = lax.rem(me, pack)
     loads = [
         pltpu.make_async_copy(src, dst, load_sem.at[i])
         for i, (src, dst) in enumerate(
             (
-                (right_in, right_own),
-                (left_in, left_own),
-                (prev_right_in, prev_right_own),
-                (prev_left_in, prev_left_own),
+                (left_in, left_got.at[my_col]),
+                (ladder_in, ladder_own),
                 (coupling_in, coupling_own),
-                (ladder_in, ladder_own),
+                (right_in, mates_got.at[my_sub, 0]),
+                (prev_right_in, mates_got.at[my_sub, 1]),
+                (prev_left_in, mates_got.at[my_sub, 2]),
             )
         )
     ]
-    for load in loads:
-        load.start()
+    home_load = pltpu.make_async_copy(right_in, right_got.at[home_slot], load_sem.at[6])
 
     def at(device):
         return (lax.div(device, cols_count), lax.rem(device, cols_count))
@@ -114,12 +111,12 @@
     for i in range(cols_count - 1):
         greet(peer(i))
 
+    for load in loads:
+        load.start()
+    pl.when(at_home)(home_load.start)
+
     lane = lax.broadcasted_iota(jnp.int32, (depth, LANES), 1)
     sub = lax.broadcasted_iota(jnp.int32, (depth, LANES), 0)
-    mine = lane // share == lax.rem(my_col, pack)
-
-    def spread(array):
-        return jnp.where(mine, jnp.concatenate([array] * pack, axis=1), 0.0)
 
     def to_lanes(columns):
         row = jnp.zeros((depth, LANES), jnp.float32)
@@ -129,18 +126,6 @@
 
     def to_column(row, i):
         return jnp.sum(jnp.where(lane == sub + i * depth, row, 0.0), axis=1, keepdims=True)
-
-    loads[0].wait()
-    loads[1].wait()
-    right = spread(right_own[...])
-    left = spread(left_own[...])
-    right_sent[0] = right
-    left_sent[0] = left
-    left_got[pl.ds(my_col, 1)] = left[None]
-
-    @pl.when(at_home)
-    def _():
-        right_got[pl.ds(home_slot, 1)] = right[None]
 
     pl.semaphore_wait(barrier, 2 * rows_count + cols_count - 1 - 2 * at_home.astype(jnp.int32))
 
@@ -155,11 +140,15 @@
         ).start()
 
     for i in (*range(1, rows_count), 0):
-        unless_me(i, lambda: send(right_sent.at[0], right_got.at[home_slot], 0, user(i)))
+        unless_me(i, lambda: send(right_in, right_got.at[home_slot], 0, user(i)))
     for i in range(cols_count - 1):
-        send(left_sent.at[0], left_got.at[my_col], 1, peer(i))
-
-    for load in loads[2:]:
+        send(left_in, left_got.at[my_col], 1, peer(i))
+    for i in range(pack - 1):
+        mate = (my_row, my_col - my_sub + lax.rem(my_sub + i + 1, pack))
+        for j, src in enumerate((right_in, prev_right_in, prev_left_in)):
+            send(src, mates_got.at[my_sub, j], 5, mate)
+
+    for load in loads:
         load.wait()
     coupling_row = coupling_own[...]
     near = lax.broadcasted_iota(jnp.int32, (depth, depth), 0) == lax.broadcasted_iota(
@@ -169,16 +158,11 @@
     def coefficient(i):
         return jnp.sum(jnp.where(near, coupling_row[i : i + 1], 0.0), axis=1, keepdims=True)
 
-    right_base = coefficient(1) * spread(prev_right_own[...])
-    left_base = coefficient(0) * spread(prev_left_own[...])
-
-    def joined(ref, count):
-        return jnp.concatenate(
-            [sum(ref[i * pack + j] for j in range(pack)) for i in range(count // pack)], axis=1
-        )
+    def joined(pieces):
+        return jnp.concatenate(pieces, axis=1)
 
     arrived(left_got, cols_count - 1, recv_sem.at[1])
-    left_rows = joined(left_got, cols_count)
+    left_rows = joined([left_got[i] for i in range(cols_count)])
     left_terms = jnp.dot(
         left_rows.astype(jnp.bfloat16), ladder_own[...], preferred_element_type=jnp.float32
     )
@@ -193,6 +177,7 @@
 
     @pl.when(at_home)
     def _():
+        home_load.wait()
         left_part_got[pl.ds(my_row, 1)] = left_part[pl.ds(lax.div(home_slot, pack), 1)]
         arrived(right_got, rows_count - 1, recv_sem.at[0])
 
@@ -200,7 +185,7 @@
     def _():
         arrived(right_got, rows_count, recv_sem.at[0])
 
-    right_cols = joined(right_got, rows_count)
+    right_cols = joined([right_got[i] for i in range(rows_count)])
     right_terms = lax.dot_general(
         right_cols.astype(jnp.bfloat16),
         ladder_own[...],
@@ -222,14 +207,20 @@
         usable = square > SMALLEST_SQUARE
         return jnp.where(usable, product / jnp.where(usable, square, 1.0), 0.0)
 
+    arrived(mates_got, pack - 1, recv_sem.at[5])
+    right, prev_right, prev_left = (
+        joined([mates_got[i, j] for i in range(pack)]) for j in range(3)
+    )
+    first_col = my_col - my_sub
+    left = joined([left_got[first_col + i] for i in range(pack)])
     right_square = inner(right, right)
     left_square = inner(left, left)
     left_right = inner(left, right)
 
     arrived(right_part_got, cols_count - 1, recv_sem.at[3])
-    image_right = jnp.where(mine, jnp.sum(right_part_got[...], axis=0), 0.0)
+    image_right = jnp.sum(right_part_got[...], axis=0)
     alpha_part = inner(left, image_right)
-    right_base = image_right - right_base
+    right_base = image_right - coefficient(1) * prev_right
     right_fit = fitted(inner(right_base, right), right_square)
     right_rest = right_base - right_fit * right
 
@@ -241,7 +232,7 @@
     def _():
         arrived(left_part_got, rows_count, recv_sem.at[2])
 
-    left_base = jnp.where(mine, jnp.sum(left_part_got[...], axis=0), 0.0) - left_base
+    left_base = jnp.sum(left_part_got[...], axis=0) - coefficient(0) * prev_left
     left_fit = fitted(inner(left_base, left), left_square)
     left_rest = left_base - left_fit * left
 
@@ -262,25 +253,32 @@
             left_right,
         ]
     )
+    low = my_group < groups // 2
+
+    def far_first(i):
+        down = groups - 1 - i
+        down = down - (down <= my_group).astype(jnp.int32)
+        up = i + (i >= my_group).astype(jnp.int32)
+        return at(jnp.where(low, down, up) * pack + my_sub)
+
     each(
-        devices - 1,
-        lambda i: send(
-            sums_sent, sums_got.at[pl.ds(me, 1)], 4, at(lax.rem(me + i + 1, devices))
-        ),
-    )
-    sums_got[pl.ds(me, 1)] = sums_sent[...]
+        groups - 1,
+        lambda i: send(sums_sent, sums_got.at[pl.ds(my_group, 1)], 4, far_first(i)),
+    )
+    sums_got[pl.ds(my_group, 1)] = sums_sent[...]
 
     arrived(right_got, rows_count - 1, send_sem.at[0])
     arrived(left_got, cols_count - 1, send_sem.at[1])
     arrived(left_part_got, rows_count - 1, send_sem.at[2])
     arrived(right_part_got, cols_count - 1, send_sem.at[3])
+    arrived(mates_got, pack - 1, send_sem.at[5])
 
     @pl.when(jnp.logical_not(at_home))
     def _():
         arrived(right_got, 1, send_sem.at[0])
         arrived(left_part_got, 1, send_sem.at[2])
 
-    arrived(sums_got, devices - 1, recv_sem.at[4])
+    arrived(sums_got, groups - 1, recv_sem.at[4])
     sums = sums_got[...]
 
     def value(i):
@@ -316,7 +314,7 @@
         out = array[:, :share]
         for i in range(1, pack):
             out = jnp.where(
-                lax.rem(my_col, pack) == i, array[:, i * share : (i + 1) * share], out
+                my_sub == i, array[:, i * share : (i + 1) * share], out
             )
         return out
 
@@ -325,7 +323,7 @@
     coefficients_out[0:1] = alpha_row[:, :depth]
     coefficients_out[1:2] = to_lanes([beta_new])[:, :depth]
     coefficients_out[2:3] = to_lanes([gamma_new])[:, :depth]
-    arrived(sums_got, devices - 1, send_sem.at[4])
+    arrived(sums_got, groups - 1, send_sem.at[4])
 
 
 def store(a_in, b_in, c_in, a_out, b_out, c_out, sem):
@@ -344,7 +342,6 @@
     devices = rows_count * cols_count
     pack = LANES // share
     f32 = jnp.float32
-    vec = pltpu.VMEM((depth, share), f32)
 
     def tiles(count):
         return pltpu.VMEM((count, depth, LANES), f32)
@@ -359,25 +356,20 @@
         in_specs=[pl.BlockSpec(memory_space=pltpu.HBM)] * 6,
         out_specs=(pl.BlockSpec(memory_space=pltpu.VMEM),) * 3,
         scratch_shapes=[
-            vec,
-            vec,
-            vec,
-            vec,
             pltpu.VMEM(coupling.shape, f32),
             pltpu.VMEM(ladder.shape, ladder.dtype),
-            tiles(1),
-            tiles(1),
-            tiles(rows_count),
-            tiles(cols_count),
+            pltpu.VMEM((rows_count, depth, share), f32),
+            pltpu.VMEM((cols_count, depth, share), f32),
+            pltpu.VMEM((pack, 3, depth, share), f32),
             tiles(cols_count // pack),
             tiles(rows_count // pack),
             tiles(cols_count),
             tiles(rows_count),
             pltpu.VMEM((1, LANES), f32),
-            pltpu.VMEM((devices, LANES), f32),
+            pltpu.VMEM((devices // pack, LANES), f32),
+            pltpu.SemaphoreType.DMA((7,)),
             pltpu.SemaphoreType.DMA((6,)),
-            pltpu.SemaphoreType.DMA((5,)),
-            pltpu.SemaphoreType.DMA((5,)),
+            pltpu.SemaphoreType.DMA((6,)),
         ],
         compiler_params=pltpu.CompilerParams(
             collective_id=0, has_side_effects=True, vmem_limit_bytes=56 * 1024 * 1024

time: 21.9 us -> 22.3 us (1.018)
  Pallas kernels: 21.1 us -> 21.5 us
    pallas_call x1, Pallas kernels: 19.7 us -> 20.1 us  [local(): pl.pallas_call(functools.partial(kernel, rows_count, cols_count), out_sha...]
where the time goes in v1:
time: 22.3 us; the launch traced here: 22.1 us
  Pallas kernels  21.5 us (96%)
  between operations  0.64 us (3%)
    pallas_call x1, Pallas kernels, local(): pl.pallas_call(functools.partial(kernel, rows_count, cols_count), out_sha...  20.1 us
    pallas_call x1, Pallas kernels, local(): pl.pallas_call(store, out_shape=tuple((jax.ShapeDtypeStruct(x.shape, x.dt...  1.43 us

profile of v1, /device:TPU:0, one launch (start us, length us, event | category | flops | bytes accessed | tf_op | source)
XLA Modules:
  0.0 22.1 jit_solution(931705154709146930)
XLA Ops:
  0.6 20.1 %shard_map.85 = (f32[8,64]{1,0:T(8,128)}, f32[8,64]{1,0:T(8,128)}, f32[3,8]{1,0:T(4,128)}) custom-call(f32[8,64]{1,0:T(8,128)} %right_in.1, f32[8,64]{1,0:T(8,128)} %left_in.1, f32[8,64]{1,0:T(8,128)} %prev_right_in.1, f32[8,64]{1,0:T(8,128)} %prev_left_in.1, f32[2,8]{1,0:T(2,128)} %coupling_in.1, bf16[256,512]{1,0:T(8,128)(2,1)} %ladder_in.1), custom_call_target="tpu_custom_call" | custom-call | tf_op jit(solution)/shard_map/pallas_call | solution.py:349
  20.7 1.4 %shard_map.86 = (f32[8,64]{1,0:T(8,128)}, f32[8,64]{1,0:T(8,128)}, f32[3,8]{1,0:T(4,128)}) custom-call(f32[8,64]{1,0:T(8,128)} %get-tuple-element.6.a_in, f32[8,64]{1,0:T(8,128)} %get-tuple-element.7.b_in, f32[3,8]{1,0:T(4,128)} %get-tuple-element.8.c_in), custom_call_target="tpu_custom_call" | custom-call | tf_op jit(solution)/shard_map/pallas_call | solution.py:378
